TPU v7x, 32 devices: a whole 2x2x4 slice. The times are simulated.
32 devices in a mesh: seq: 16 (over z, y, x), chan: 2 (over core).
Axes of the slice: x: 2, y: 2, z: 4, core: 2. Of those that a mesh axis runs over, the one named last changes fastest.
Arguments:
- streams: bfloat16 [3, 512, 4096], P(None, 'chan', 'seq'), may hold values from -6 to 6
- short_filters: float32 [3, 7, 512], P(None, None, 'chan'), may hold values from -2 to 2
- long_filter: float32 [64, 4096], P(None, 'seq'), may hold values from -2 to 2
- skip_gain: float32 [512], P('chan'), may hold values from 0.3 to 1.5
- out_grad: bfloat16 [512, 4096], P('chan', 'seq'), may hold values from -6 to 6
Outputs:
- stream_grad: bfloat16 [3, 512, 4096], P(None, 'chan', 'seq')
- filter_grad: float32 [64, 4096], P(None, 'seq')
All inputs are finite; a program needn't handle non-finite values.
Results may differ from a plain program's by a relative error of at most 0.0004.
Values may be sent and summed in bfloat16 or wider, within the bound.
A program may use at most 64 MiB of HBM per device.

v0:
```python
import math
import jax
import jax.numpy as jnp
from jax import lax
from jax.sharding import PartitionSpec as P


def partner_2(value, axis, apart):
    mask = 2**apart
    pairs = [(source, source ^ mask) for source in range(lax.axis_size(axis))]
    return lax.ppermute(value, axis, pairs)


def shifted(shard, axis, by):
    length = lax.axis_size(axis)
    pairs = [(i, i + by) for i in range(length) if 0 <= i + by < length]
    return lax.ppermute(shard, axis, pairs)


def rotate(real_part, imag_part, cosine, sine_part):
    return (real_part * cosine - imag_part * sine_part, real_part * sine_part + imag_part * cosine)


def split_halves(signal):
    middle = signal.shape[-1] // 2
    return (signal[..., :middle], signal[..., middle:])


def join_halves(real_part, imag_part):
    return jnp.concatenate([real_part, imag_part], axis=-1)


def complex_product(first_op, second_op, conjugate):
    first_re, first_im = split_halves(first_op)
    second_re, second_im = split_halves(second_op)
    if conjugate:
        second_im = -second_im
    return join_halves(
        first_re * second_re - first_im * second_im, first_re * second_im + first_im * second_re
    )


def dft_table(length, direction, scaling):
    indices = jnp.arange(length, dtype=jnp.int32)
    phases = (indices[:, None] * indices[None, :] % length).astype(jnp.float32) * (
        direction * 2.0 * math.pi / length
    )
    cosine = jnp.cos(phases) * scaling
    sine_part = jnp.sin(phases) * scaling
    upper_rows = jnp.concatenate([cosine, sine_part], axis=1)
    lower_rows = jnp.concatenate([-sine_part, cosine], axis=1)
    return jnp.concatenate([upper_rows, lower_rows], axis=0)


def section_count():
    return lax.axis_size("seq").bit_length() - 1


def bit_reverse(position, sections):
    result = jnp.zeros((), jnp.int32)
    for bit_level in range(sections):
        result = result + position // (1 << bit_level) % 2 * (1 << sections - 1 - bit_level)
    return result


def held_index():
    return bit_reverse(lax.axis_index("seq"), section_count())


def inner_twiddle(signal, held, direction):
    length = signal.shape[-1] // 2
    seq_total = length * lax.axis_size("seq")
    indices = jnp.arange(length, dtype=jnp.int32)
    phases = (indices * held % seq_total).astype(jnp.float32) * (
        direction * 2.0 * math.pi / seq_total
    )
    real_part, imag_part = split_halves(signal)
    turned_re, turned_im = rotate(real_part, imag_part, jnp.cos(phases), jnp.sin(phases))
    return join_halves(turned_re, turned_im)


def forward_sections(signal):
    position = lax.axis_index("seq")
    sections = section_count()
    for bit_level in reversed(range(sections)):
        half_span = 1 << bit_level
        partner = partner_2(signal, "seq", bit_level)
        upper_side = position // half_span % 2 == 1
        phases = (position % half_span).astype(jnp.float32) * (-math.pi / half_span)
        diff_re, diff_im = split_halves(partner - signal)
        turned_re, turned_im = rotate(diff_re, diff_im, jnp.cos(phases), jnp.sin(phases))
        signal = jnp.where(upper_side, join_halves(turned_re, turned_im), signal + partner)
    return signal


def inverse_sections(signal):
    position = lax.axis_index("seq")
    sections = section_count()
    for bit_level in range(sections):
        half_span = 1 << bit_level
        partner = partner_2(signal, "seq", bit_level)
        upper_side = position // half_span % 2 == 1
        phases = (position % half_span).astype(jnp.float32) * (math.pi / half_span)
        source = jnp.where(upper_side, signal, partner)
        base_term = jnp.where(upper_side, partner, signal)
        source_re, source_im = split_halves(source)
        turned_re, turned_im = rotate(source_re, source_im, jnp.cos(phases), jnp.sin(phases))
        turned = join_halves(turned_re, turned_im)
        signal = 0.5 * jnp.where(upper_side, base_term - turned, base_term + turned)
    return signal


def forward_dft(signal, dft_matrix):
    signal = forward_sections(signal)
    signal = inner_twiddle(signal, held_index(), -1.0)
    return jnp.dot(
        signal, dft_matrix, precision=lax.Precision.HIGHEST, preferred_element_type=jnp.float32
    )


def inverse_dft(spectra, dft_matrix):
    signal = jnp.dot(
        spectra, dft_matrix, precision=lax.Precision.HIGHEST, preferred_element_type=jnp.float32
    )
    signal = inner_twiddle(signal, held_index(), 1.0)
    return inverse_sections(signal)


def local(streams, short_filters, long_filter, skip_gain, out_grad):
    tap_count = short_filters.shape[1]
    reach_back = tap_count - 1
    channels_dev = streams.shape[1]
    length = streams.shape[2]
    filters = long_filter.shape[0]
    members = channels_dev // filters
    devices = lax.axis_size("seq")
    position = lax.axis_index("seq")
    seq_total = length * devices
    preceding = shifted(streams[:, :, length - reach_back :], "seq", 1)
    extended = jnp.concatenate([preceding, streams], axis=2).astype(jnp.float32)
    filtered = jnp.zeros(streams.shape, jnp.float32)
    for offset in range(tap_count):
        filtered = (
            filtered
            + short_filters[:, offset, :, None]
            * extended[:, :, reach_back - offset : reach_back - offset + length]
        )
    gate_out = filtered[0]
    gate_in = filtered[1]
    values = filtered[2]
    gated_prod = gate_in * values
    out_float = out_grad.astype(jnp.float32)
    gate_grad = out_float * gate_out
    signals = jnp.concatenate([gated_prod, gate_grad, long_filter], axis=0)
    twist_phase = (position * length + jnp.arange(length, dtype=jnp.int32)).astype(jnp.float32) * (
        -math.pi / seq_total
    )
    twist_re = jnp.cos(twist_phase)
    twist_im = jnp.sin(twist_phase)
    even_part = join_halves(signals, jnp.zeros_like(signals))
    odd_part = join_halves(signals * twist_re, signals * twist_im)
    spectra = forward_dft(
        jnp.concatenate([even_part, odd_part], axis=0), dft_table(length, -1.0, 1.0)
    )
    row_count = signals.shape[0]
    halves = (spectra[:row_count], spectra[row_count:])
    filter_specs = (halves[0][2 * channels_dev :], halves[1][2 * channels_dev :])
    products = []
    for half_index in range(2):
        part_spec = halves[half_index]
        gated_spec = part_spec[:channels_dev]
        grad_spec = part_spec[channels_dev : 2 * channels_dev]
        wide_filter = jnp.tile(filter_specs[half_index], (members, 1))
        products.append(complex_product(gated_spec, wide_filter, False))
        products.append(complex_product(grad_spec, wide_filter, True))
        products.append(
            complex_product(grad_spec, gated_spec, True)
            .reshape(members, filters, 2 * length)
            .sum(axis=0)
        )
    time_rows = inverse_dft(jnp.concatenate(products, axis=0), dft_table(length, 1.0, 1.0 / length))
    part_rows = 2 * channels_dev + filters
    even_re, even_im = split_halves(time_rows[:part_rows])
    odd_re, odd_im = split_halves(time_rows[part_rows:])
    combined = 0.5 * (even_re + twist_re * odd_re + twist_im * odd_im)
    conv_part = combined[:channels_dev]
    corr_part = combined[channels_dev : 2 * channels_dev]
    filter_local = combined[2 * channels_dev :]
    conv_out = conv_part + skip_gain[:, None] * gated_prod
    gated_grad = corr_part + skip_gain[:, None] * gate_grad
    members_total = channels_dev * lax.axis_size("chan") // filters
    filter_grad = lax.psum(filter_local, "chan") * (1.0 / math.sqrt(members_total * seq_total))
    grads_in = jnp.stack([out_float * conv_out, gated_grad * values, gated_grad * gate_in])
    following = shifted(grads_in[:, :, :reach_back], "seq", -1)
    extended_grad = jnp.concatenate([grads_in, following], axis=2)
    result = jnp.zeros(grads_in.shape, jnp.float32)
    for offset in range(tap_count):
        result = (
            result
            + short_filters[:, offset, :, None] * extended_grad[:, :, offset : offset + length]
        )
    return (result.astype(jnp.bfloat16), filter_grad)


def solution(mesh):
    in_specs = (
        P(None, "chan", "seq"),
        P(None, None, "chan"),
        P(None, "seq"),
        P("chan"),
        P("chan", "seq"),
    )
    out_specs = (P(None, "chan", "seq"), P(None, "seq"))
    return jax.shard_map(local, mesh=mesh, in_specs=in_specs, out_specs=out_specs, check_vma=False)
```

profile of v0, /device:TPU:0, one launch (start us, length us, event | category | flops | bytes accessed | tf_op | source)
XLA Modules:
  0.0 611.4 jit_solution(11527315104026521100)
XLA Ops:
  7.2 1.2 copy.14
  8.4 4.8 collective-permute-start
  13.2 1.0 fusion.52
  14.4 1.0 copy.13
  15.4 1.0 copy.16
  17.5 1.9 select_maximum_fusion
  19.4 3.4 collective-permute-start.1
  23.0 100.9 %collective-permute-done.1 = f32[1152,512]{0,1:T(8,128)} collective-permute-done((f32[1152,512]{0,1:T(8,128)}, f32[1152,512]{0,1:T(8,128)}, u32[]{:S(2)}, u32[]{:S(2)}) %collective-permute-start.1) | collective-permute-done | bytes 2359328 | tf_op jit(solution)/shard_map/ppermute | solution.py:11
  123.9 2.1 fusion.50
  126.3 2.5 maximum_select_fusion
  129.7 51.3 %collective-permute-done.2 = f32[1152,512]{0,1:T(8,128)} collective-permute-done((f32[1152,512]{0,1:T(8,128)S(1)}, f32[1152,512]{0,1:T(8,128)}, u32[]{:S(2)}, u32[]{:S(2)}) %collective-permute-start.2) | collective-permute-done | bytes 2359328 | tf_op jit(solution)/shard_map/ppermute | solution.py:11
  181.0 1.9 sub.100
  183.2 3.5 maximum_select_fusion.1
  186.7 1.5 collective-permute-start.3
  188.4 50.0 %collective-permute-done.3 = f32[1152,512]{0,1:T(8,128)S(1)} collective-permute-done((f32[1152,512]{0,1:T(8,128)}, f32[1152,512]{0,1:T(8,128)S(1)}, u32[]{:S(2)}, u32[]{:S(2)}) %collective-permute-start.3) | collective-permute-done | bytes 2359328 | tf_op jit(solution)/shard_map/ppermute | solution.py:11
  238.4 2.8 sub.102
  241.4 2.8 maximum_select_fusion.2
  244.2 1.6 collective-permute-start.4
  246.5 1.0 fusion.42
  247.5 1.7 fusion.43
  249.2 1.0 multiply_sine_fusion
  250.2 1.8 sine_multiply_fusion
  252.0 42.9 %collective-permute-done.4 = f32[1152,512]{0,1:T(8,128)} collective-permute-done((f32[1152,512]{0,1:T(8,128)S(1)}, f32[1152,512]{0,1:T(8,128)}, u32[]{:S(2)}, u32[]{:S(2)}) %collective-permute-start.4) | collective-permute-done | bytes 2359328 | tf_op jit(solution)/shard_map/ppermute | solution.py:11
  295.0 1.9 sub.104
  297.0 2.1 maximum_select_fusion.3
  299.5 4.0 fusion
  303.5 0.9 multiply_subtract_fusion.10
  304.5 1.0 multiply_subtract_fusion.11
  306.3 1.1 pad_maximum_fusion.8
  309.7 4.8 fusion.11
  315.0 1.6 collective-permute-start.5
  316.6 48.1 %collective-permute-done.5 = f32[1152,512]{0,1:T(8,128)S(1)} collective-permute-done((f32[1152,512]{0,1:T(8,128)S(1)}, f32[1152,512]{0,1:T(8,128)S(1)}, u32[]{:S(2)}, u32[]{:S(2)}) %collective-permute-start.5) | collective-permute-done | bytes 2359328 | tf_op jit(solution)/shard_map/ppermute | solution.py:11
  365.8 1.6 collective-permute-start.6
  367.5 47.1 %collective-permute-done.6 = f32[1152,512]{0,1:T(8,128)} collective-permute-done((f32[1152,512]{0,1:T(8,128)S(1)}, f32[1152,512]{0,1:T(8,128)}, u32[]{:S(2)}, u32[]{:S(2)}) %collective-permute-start.6) | collective-permute-done | bytes 2359328 | tf_op jit(solution)/shard_map/ppermute | solution.py:11
  414.6 1.9 broadcast_select_fusion.1
  416.8 1.8 select_multiply_fusion.2
  418.6 5.1 collective-permute-start.7
  423.9 46.9 %collective-permute-done.7 = f32[1152,512]{0,1:T(8,128)S(1)} collective-permute-done((f32[1152,512]{0,1:T(8,128)}, f32[1152,512]{0,1:T(8,128)S(1)}, u32[]{:S(2)}, u32[]{:S(2)}) %collective-permute-start.7) | collective-permute-done | bytes 2359328 | tf_op jit(solution)/shard_map/ppermute | solution.py:11
  471.1 1.2 copy-done.3
  472.6 2.1 select_multiply_fusion.1
  474.6 5.0 collective-permute-start.8
  479.8 96.8 %collective-permute-done.8 = f32[1152,512]{0,1:T(8,128)} collective-permute-done((f32[1152,512]{0,1:T(8,128)S(1)}, f32[1152,512]{0,1:T(8,128)}, u32[]{:S(2)}, u32[]{:S(2)}) %collective-permute-start.8) | collective-permute-done | bytes 2359328 | tf_op jit(solution)/shard_map/ppermute | solution.py:11
  576.6 1.9 broadcast_select_fusion.3
  580.8 1.3 collective-permute-start.9
  582.8 3.7 collective-permute-done.9
  587.3 0.9 copy.17
  588.2 14.7 %all-reduce.3.cloned.1.call-done = f32[64,256]{0,1:T(8,128)} async-done(((f32[64,256]{0,1:T(8,128)}), f32[64,256]{0,1:T(8,128)}) %all-reduce.3.cloned.1.call-update) | async-done | bytes 65552 | tf_op jit(solution)/shard_map/psum | solution.py:192
  602.9 0.9 broadcast_multiply_fusion.2
  (111 shorter events, 13.4 us)
Async XLA Ops:
  7.2 595.8 %all-reduce.3.cloned.1.call-start = ((), (), s32[]{:S(2)}) async-start(), calls=%async_computation | async-start | bytes 262144 | tf_op jit(solution)/shard_map/psum | solution.py:192
  8.4 8.0 %collective-permute-start = (bf16[3,256,6]{1,2,0:T(8,128)(2,1)S(1)}, bf16[3,256,6]{1,2,0:T(8,128)(2,1)S(1)}, u32[]{:S(2)}, u32[]{:S(2)}) collective-permute-start(bf16[3,256,6]{1,2,0:T(8,128)(2,1)S(1)} %slice.304), channel_id=1, source_target_pairs={{0,2},{2,4},{4,6},{6,8},{8,10},{10,12},{12,14},{14,16},{16,18},{18... | collective-permute-start | bytes 27656 | tf_op jit(solution)/shard_map/ppermute | solution.py:17
  14.3 2.9 copy-start.17
  14.3 2.9 copy-start.19
  14.4 2.9 copy-start.23
  14.4 2.9 copy-start.25
  14.4 2.8 copy-start.21
  15.4 1.8 copy-start.6
  17.2 2.2 copy-start.4
  17.5 108.5 %copy-start = (f32[576,256]{0,1:T(8,128)}, f32[576,256]{0,1:T(8,128)S(1)}, u32[]{:S(2)}) copy-start(f32[576,256]{0,1:T(8,128)S(1)} %get-tuple-element.46) | copy-start | bytes 1769476
  17.5 108.5 %copy-start.1 = (f32[576,256]{0,1:T(8,128)}, f32[576,256]{0,1:T(8,128)S(1)}, u32[]{:S(2)}) copy-start(f32[576,256]{0,1:T(8,128)S(1)} %get-tuple-element.47) | copy-start | bytes 1769476
  19.4 104.5 %collective-permute-start.1 = (f32[1152,512]{0,1:T(8,128)}, f32[1152,512]{0,1:T(8,128)}, u32[]{:S(2)}, u32[]{:S(2)}) collective-permute-start(f32[1152,512]{0,1:T(8,128)} %select_maximum_fusion), channel_id=1, source_target_pairs={{0,16},{2,18},{4,20},{6,22},{8,24},{10,26},{12,28},{14,30},{16,0},... | collective-permute-start | bytes 7077896 | tf_op jit(solution)/shard_map/ppermute | solution.py:11
  128.8 52.3 %collective-permute-start.2 = (f32[1152,512]{0,1:T(8,128)S(1)}, f32[1152,512]{0,1:T(8,128)}, u32[]{:S(2)}, u32[]{:S(2)}) collective-permute-start(f32[1152,512]{0,1:T(8,128)S(1)} %maximum_select_fusion), channel_id=1, source_target_pairs={{0,8},{2,10},{4,12},{6,14},{8,0},{10,2},{12,4},{14,6},{16,24},{18,... | collective-permute-start | bytes 7077896 | tf_op jit(solution)/shard_map/ppermute | solution.py:11
  186.7 51.7 %collective-permute-start.3 = (f32[1152,512]{0,1:T(8,128)}, f32[1152,512]{0,1:T(8,128)S(1)}, u32[]{:S(2)}, u32[]{:S(2)}) collective-permute-start(f32[1152,512]{0,1:T(8,128)} %maximum_select_fusion.1), channel_id=1, source_target_pairs={{0,4},{2,6},{4,0},{6,2},{8,12},{10,14},{12,8},{14,10},{16,20},{18,... | collective-permute-start | bytes 7077896 | tf_op jit(solution)/shard_map/ppermute | solution.py:11
  238.4 2.8 copy-start.2
  244.2 50.7 %collective-permute-start.4 = (f32[1152,512]{0,1:T(8,128)S(1)}, f32[1152,512]{0,1:T(8,128)}, u32[]{:S(2)}, u32[]{:S(2)}) collective-permute-start(f32[1152,512]{0,1:T(8,128)S(1)} %maximum_select_fusion.2), channel_id=1, source_target_pairs={{0,2},{2,0},{4,6},{6,4},{8,10},{10,8},{12,14},{14,12},{16,18},{18,... | collective-permute-start | bytes 7077896 | tf_op jit(solution)/shard_map/ppermute | solution.py:11
  308.1 0.9 copy-start.16
  308.1 1.0 copy-start.10
  308.2 1.1 copy-start.11
  308.3 1.0 copy-start.8
  308.3 1.1 copy-start.9
  308.3 1.2 copy-start.15
  308.3 1.2 copy-start.12
  308.3 1.3 copy-start.13
  308.3 1.4 copy-start.14
  309.7 4.8 copy-start.27
  309.7 4.8 copy-start.28
  315.0 49.7 %collective-permute-start.5 = (f32[1152,512]{0,1:T(8,128)S(1)}, f32[1152,512]{0,1:T(8,128)S(1)}, u32[]{:S(2)}, u32[]{:S(2)}) collective-permute-start(f32[1152,512]{0,1:T(8,128)S(1)} %pad_maximum_fusion), channel_id=1, source_target_pairs={{0,2},{2,0},{4,6},{6,4},{8,10},{10,8},{12,14},{14,12},{16,18},{18,... | collective-permute-start | bytes 7077896 | tf_op jit(solution)/shard_map/ppermute | solution.py:11
  365.8 48.9 %collective-permute-start.6 = (f32[1152,512]{0,1:T(8,128)S(1)}, f32[1152,512]{0,1:T(8,128)}, u32[]{:S(2)}, u32[]{:S(2)}) collective-permute-start(f32[1152,512]{0,1:T(8,128)S(1)} %select_multiply_fusion.3), channel_id=1, source_target_pairs={{0,4},{2,6},{4,0},{6,2},{8,12},{10,14},{12,8},{14,10},{16,20},{18,... | collective-permute-start | bytes 7077896 | tf_op jit(solution)/shard_map/ppermute | solution.py:11
  418.6 52.2 %collective-permute-start.7 = (f32[1152,512]{0,1:T(8,128)}, f32[1152,512]{0,1:T(8,128)S(1)}, u32[]{:S(2)}, u32[]{:S(2)}) collective-permute-start(f32[1152,512]{0,1:T(8,128)} %select_multiply_fusion.2), channel_id=1, source_target_pairs={{0,8},{2,10},{4,12},{6,14},{8,0},{10,2},{12,4},{14,6},{16,24},{18,... | collective-permute-start | bytes 7077896 | tf_op jit(solution)/shard_map/ppermute | solution.py:11
  470.8 1.5 copy-start.3
  474.6 102.0 %collective-permute-start.8 = (f32[1152,512]{0,1:T(8,128)S(1)}, f32[1152,512]{0,1:T(8,128)}, u32[]{:S(2)}, u32[]{:S(2)}) collective-permute-start(f32[1152,512]{0,1:T(8,128)S(1)} %select_multiply_fusion.1), channel_id=1, source_target_pairs={{0,16},{2,18},{4,20},{6,22},{8,24},{10,26},{12,28},{14,30},{16,0},... | collective-permute-start | bytes 7077896 | tf_op jit(solution)/shard_map/ppermute | solution.py:11
  578.8 0.7 copy-start.24
  578.8 0.7 copy-start.26
  579.5 1.1 copy-start.5
  579.5 1.1 copy-start.7
  579.5 1.1 copy-start.29
  580.7 5.9 copy-start.18
  580.7 5.9 copy-start.20
  580.7 5.9 copy-start.22
  580.8 5.7 collective-permute-start.9
Sparse Core Ops, SparseCore 0:
  582.9 19.9 all-reduce.2
where the time goes:
time: 612 us; the launch traced here: 611 us
  waiting for transfers between devices  503 us (82%)
  other arithmetic  47.7 us (8%)
  starting transfers between devices  26.7 us (4%)
  between operations  15.8 us (3%)
  local copies, waits for them, and re-layouts  9.85 us (2%)
  matrix products  8.79 us (1%)
    ppermute x8, waiting for transfers between devices, partner_2(): return lax.ppermute(value, axis, pairs)  484 us
    ppermute x8, starting transfers between devices, partner_2(): return lax.ppermute(value, axis, pairs)  20.5 us
    psum x1, waiting for transfers between devices, local(): lax.psum(filter_local, 'chan')  14.7 us
  transfers between devices with their start and end apart: 11, of which 10 were waited for; matrix products, arithmetic and copies ran while one was open for 2% of the time, Pallas kernels for 0%

commit v1 on v0

--- a/solution.py
+++ b/solution.py
@@ -189,7 +189,9 @@
     conv_out = conv_part + skip_gain[:, None] * gated_prod
     gated_grad = corr_part + skip_gain[:, None] * gate_grad
     members_total = channels_dev * lax.axis_size("chan") // filters
-    filter_grad = lax.psum(filter_local, "chan") * (1.0 / math.sqrt(members_total * seq_total))
+    filter_grad = jnp.sum(lax.all_gather(filter_local, "chan"), axis=0) * (
+        1.0 / math.sqrt(members_total * seq_total)
+    )
     grads_in = jnp.stack([out_float * conv_out, gated_grad * values, gated_grad * gate_in])
     following = shifted(grads_in[:, :, :reach_back], "seq", -1)
     extended_grad = jnp.concatenate([grads_in, following], axis=2)

time: 612 us -> 583 us (0.953)
  waiting for transfers between devices: 503 us -> 486 us
  between operations: 15.8 us -> 2.41 us
    psum x1 -> x0, waiting for transfers between devices: 14.7 us -> none  [local(): lax.psum(filter_local, 'chan')]
  transfers between devices with their start and end apart: 11 -> 10, of which waited for: 10 -> 9; matrix products, arithmetic and copies ran while one was open for 2% -> 2% of each run, Pallas kernels for 0% -> 0%
where the time goes in v1:
time: 583 us; the launch traced here: 582 us
  waiting for transfers between devices  486 us (83%)
  other arithmetic  47.4 us (8%)
  starting transfers between devices  26.6 us (5%)
  matrix products  8.79 us (2%)
  local copies, waits for them, and re-layouts  8.57 us (1%)
    ppermute x8, waiting for transfers between devices, partner_2(): return lax.ppermute(value, axis, pairs)  484 us
    ppermute x8, starting transfers between devices, partner_2(): return lax.ppermute(value, axis, pairs)  20.5 us
  transfers between devices with their start and end apart: 10, of which 9 were waited for; matrix products, arithmetic and copies ran while one was open for 2% of the time, Pallas kernels for 0%

profile of v1, /device:TPU:0, one launch (start us, length us, event | category | flops | bytes accessed | tf_op | source)
XLA Modules:
  0.0 581.7 jit_solution(15868399910879631035)
XLA Ops:
  0.6 1.2 copy.19
  1.8 4.8 collective-permute-start
  6.7 1.0 fusion.52
  7.8 1.0 copy.18
  8.9 1.0 copy.21
  10.9 1.9 select_maximum_fusion
  12.8 3.4 collective-permute-start.1
  16.4 100.9 %collective-permute-done.1 = f32[1152,512]{0,1:T(8,128)} collective-permute-done((f32[1152,512]{0,1:T(8,128)}, f32[1152,512]{0,1:T(8,128)}, u32[]{:S(2)}, u32[]{:S(2)}) %collective-permute-start.1) | collective-permute-done | bytes 2359328 | tf_op jit(solution)/shard_map/ppermute | solution.py:11
  117.3 2.1 fusion.50
  119.7 2.5 maximum_select_fusion
  122.2 0.7 collective-permute-start.2
  123.1 51.3 %collective-permute-done.2 = f32[1152,512]{0,1:T(8,128)} collective-permute-done((f32[1152,512]{0,1:T(8,128)S(1)}, f32[1152,512]{0,1:T(8,128)}, u32[]{:S(2)}, u32[]{:S(2)}) %collective-permute-start.2) | collective-permute-done | bytes 2359328 | tf_op jit(solution)/shard_map/ppermute | solution.py:11
  174.5 1.9 sub.100
  176.6 3.5 maximum_select_fusion.1
  180.1 1.5 collective-permute-start.3
  181.9 50.0 %collective-permute-done.3 = f32[1152,512]{0,1:T(8,128)S(1)} collective-permute-done((f32[1152,512]{0,1:T(8,128)}, f32[1152,512]{0,1:T(8,128)S(1)}, u32[]{:S(2)}, u32[]{:S(2)}) %collective-permute-start.3) | collective-permute-done | bytes 2359328 | tf_op jit(solution)/shard_map/ppermute | solution.py:11
  231.8 2.8 sub.102
  234.9 2.8 maximum_select_fusion.2
  237.7 1.6 collective-permute-start.4
  239.9 1.0 fusion.42
  240.9 1.7 fusion.43
  242.6 1.0 multiply_sine_fusion
  243.6 1.8 sine_multiply_fusion
  245.4 43.0 %collective-permute-done.4 = f32[1152,512]{0,1:T(8,128)} collective-permute-done((f32[1152,512]{0,1:T(8,128)S(1)}, f32[1152,512]{0,1:T(8,128)}, u32[]{:S(2)}, u32[]{:S(2)}) %collective-permute-start.4) | collective-permute-done | bytes 2359328 | tf_op jit(solution)/shard_map/ppermute | solution.py:11
  288.4 1.9 sub.104
  290.5 2.1 maximum_select_fusion.3
  292.9 4.0 fusion
  297.0 0.9 multiply_subtract_fusion.10
  297.9 1.0 multiply_subtract_fusion.11
  299.8 1.1 pad_maximum_fusion.8
  303.2 4.8 fusion.11
  308.5 1.6 collective-permute-start.5
  310.0 48.1 %collective-permute-done.5 = f32[1152,512]{0,1:T(8,128)S(1)} collective-permute-done((f32[1152,512]{0,1:T(8,128)S(1)}, f32[1152,512]{0,1:T(8,128)S(1)}, u32[]{:S(2)}, u32[]{:S(2)}) %collective-permute-start.5) | collective-permute-done | bytes 2359328 | tf_op jit(solution)/shard_map/ppermute | solution.py:11
  359.2 1.6 collective-permute-start.6
  361.0 47.1 %collective-permute-done.6 = f32[1152,512]{0,1:T(8,128)} collective-permute-done((f32[1152,512]{0,1:T(8,128)S(1)}, f32[1152,512]{0,1:T(8,128)}, u32[]{:S(2)}, u32[]{:S(2)}) %collective-permute-start.6) | collective-permute-done | bytes 2359328 | tf_op jit(solution)/shard_map/ppermute | solution.py:11
  408.1 1.9 broadcast_select_fusion.1
  410.3 1.8 select_multiply_fusion.2
  412.1 5.1 collective-permute-start.7
  417.4 46.9 %collective-permute-done.7 = f32[1152,512]{0,1:T(8,128)S(1)} collective-permute-done((f32[1152,512]{0,1:T(8,128)}, f32[1152,512]{0,1:T(8,128)S(1)}, u32[]{:S(2)}, u32[]{:S(2)}) %collective-permute-start.7) | collective-permute-done | bytes 2359328 | tf_op jit(solution)/shard_map/ppermute | solution.py:11
  464.6 1.2 copy-done.3
  466.0 2.1 select_multiply_fusion.1
  468.1 5.0 collective-permute-start.8
  473.3 96.8 %collective-permute-done.8 = f32[1152,512]{0,1:T(8,128)} collective-permute-done((f32[1152,512]{0,1:T(8,128)S(1)}, f32[1152,512]{0,1:T(8,128)}, u32[]{:S(2)}, u32[]{:S(2)}) %collective-permute-start.8) | collective-permute-done | bytes 2359328 | tf_op jit(solution)/shard_map/ppermute | solution.py:11
  570.1 1.9 broadcast_select_fusion.3
  574.3 1.3 collective-permute-start.9
  575.7 1.9 all-gather
  578.3 1.8 collective-permute-done.9
  580.8 0.9 copy.23
  (110 shorter events, 11.9 us)
Async XLA Ops:
  1.8 8.0 %collective-permute-start = (bf16[3,256,6]{1,2,0:T(8,128)(2,1)S(1)}, bf16[3,256,6]{1,2,0:T(8,128)(2,1)S(1)}, u32[]{:S(2)}, u32[]{:S(2)}) collective-permute-start(bf16[3,256,6]{1,2,0:T(8,128)(2,1)S(1)} %slice.304), channel_id=1, source_target_pairs={{0,2},{2,4},{4,6},{6,8},{8,10},{10,12},{12,14},{14,16},{16,18},{18... | collective-permute-start | bytes 27656 | tf_op jit(solution)/shard_map/ppermute | solution.py:17
  7.7 2.9 copy-start.17
  7.7 2.9 copy-start.19
  7.8 2.9 copy-start.23
  7.8 2.9 copy-start.25
  7.8 2.8 copy-start.21
  8.8 1.8 copy-start.6
  10.6 2.2 copy-start.4
  10.9 108.5 %copy-start = (f32[576,256]{0,1:T(8,128)}, f32[576,256]{0,1:T(8,128)S(1)}, u32[]{:S(2)}) copy-start(f32[576,256]{0,1:T(8,128)S(1)} %get-tuple-element.48) | copy-start | bytes 1769476
  10.9 108.5 %copy-start.1 = (f32[576,256]{0,1:T(8,128)}, f32[576,256]{0,1:T(8,128)S(1)}, u32[]{:S(2)}) copy-start(f32[576,256]{0,1:T(8,128)S(1)} %get-tuple-element.49) | copy-start | bytes 1769476
  12.8 104.5 %collective-permute-start.1 = (f32[1152,512]{0,1:T(8,128)}, f32[1152,512]{0,1:T(8,128)}, u32[]{:S(2)}, u32[]{:S(2)}) collective-permute-start(f32[1152,512]{0,1:T(8,128)} %select_maximum_fusion), channel_id=1, source_target_pairs={{0,16},{2,18},{4,20},{6,22},{8,24},{10,26},{12,28},{14,30},{16,0},... | collective-permute-start | bytes 7077896 | tf_op jit(solution)/shard_map/ppermute | solution.py:11
  122.2 52.3 %collective-permute-start.2 = (f32[1152,512]{0,1:T(8,128)S(1)}, f32[1152,512]{0,1:T(8,128)}, u32[]{:S(2)}, u32[]{:S(2)}) collective-permute-start(f32[1152,512]{0,1:T(8,128)S(1)} %maximum_select_fusion), channel_id=1, source_target_pairs={{0,8},{2,10},{4,12},{6,14},{8,0},{10,2},{12,4},{14,6},{16,24},{18,... | collective-permute-start | bytes 7077896 | tf_op jit(solution)/shard_map/ppermute | solution.py:11
  180.1 51.7 %collective-permute-start.3 = (f32[1152,512]{0,1:T(8,128)}, f32[1152,512]{0,1:T(8,128)S(1)}, u32[]{:S(2)}, u32[]{:S(2)}) collective-permute-start(f32[1152,512]{0,1:T(8,128)} %maximum_select_fusion.1), channel_id=1, source_target_pairs={{0,4},{2,6},{4,0},{6,2},{8,12},{10,14},{12,8},{14,10},{16,20},{18,... | collective-permute-start | bytes 7077896 | tf_op jit(solution)/shard_map/ppermute | solution.py:11
  231.8 2.8 copy-start.2
  237.7 50.7 %collective-permute-start.4 = (f32[1152,512]{0,1:T(8,128)S(1)}, f32[1152,512]{0,1:T(8,128)}, u32[]{:S(2)}, u32[]{:S(2)}) collective-permute-start(f32[1152,512]{0,1:T(8,128)S(1)} %maximum_select_fusion.2), channel_id=1, source_target_pairs={{0,2},{2,0},{4,6},{6,4},{8,10},{10,8},{12,14},{14,12},{16,18},{18,... | collective-permute-start | bytes 7077896 | tf_op jit(solution)/shard_map/ppermute | solution.py:11
  301.6 0.9 copy-start.16
  301.6 1.0 copy-start.10
  301.6 1.1 copy-start.11
  301.7 1.0 copy-start.8
  301.8 1.1 copy-start.9
  301.8 1.2 copy-start.15
  301.8 1.2 copy-start.12
  301.8 1.3 copy-start.13
  301.8 1.4 copy-start.14
  303.2 4.8 copy-start.27
  303.2 4.8 copy-start.28
  308.5 49.7 %collective-permute-start.5 = (f32[1152,512]{0,1:T(8,128)S(1)}, f32[1152,512]{0,1:T(8,128)S(1)}, u32[]{:S(2)}, u32[]{:S(2)}) collective-permute-start(f32[1152,512]{0,1:T(8,128)S(1)} %pad_maximum_fusion), channel_id=1, source_target_pairs={{0,2},{2,0},{4,6},{6,4},{8,10},{10,8},{12,14},{14,12},{16,18},{18,... | collective-permute-start | bytes 7077896 | tf_op jit(solution)/shard_map/ppermute | solution.py:11
  359.2 48.9 %collective-permute-start.6 = (f32[1152,512]{0,1:T(8,128)S(1)}, f32[1152,512]{0,1:T(8,128)}, u32[]{:S(2)}, u32[]{:S(2)}) collective-permute-start(f32[1152,512]{0,1:T(8,128)S(1)} %select_multiply_fusion.3), channel_id=1, source_target_pairs={{0,4},{2,6},{4,0},{6,2},{8,12},{10,14},{12,8},{14,10},{16,20},{18,... | collective-permute-start | bytes 7077896 | tf_op jit(solution)/shard_map/ppermute | solution.py:11
  412.1 52.2 %collective-permute-start.7 = (f32[1152,512]{0,1:T(8,128)}, f32[1152,512]{0,1:T(8,128)S(1)}, u32[]{:S(2)}, u32[]{:S(2)}) collective-permute-start(f32[1152,512]{0,1:T(8,128)} %select_multiply_fusion.2), channel_id=1, source_target_pairs={{0,8},{2,10},{4,12},{6,14},{8,0},{10,2},{12,4},{14,6},{16,24},{18,... | collective-permute-start | bytes 7077896 | tf_op jit(solution)/shard_map/ppermute | solution.py:11
  464.3 1.5 copy-start.3
  468.1 102.0 %collective-permute-start.8 = (f32[1152,512]{0,1:T(8,128)S(1)}, f32[1152,512]{0,1:T(8,128)}, u32[]{:S(2)}, u32[]{:S(2)}) collective-permute-start(f32[1152,512]{0,1:T(8,128)S(1)} %select_multiply_fusion.1), channel_id=1, source_target_pairs={{0,16},{2,18},{4,20},{6,22},{8,24},{10,26},{12,28},{14,30},{16,0},... | collective-permute-start | bytes 7077896 | tf_op jit(solution)/shard_map/ppermute | solution.py:11
  572.3 0.6 copy-start.24
  572.3 0.7 copy-start.26
  573.0 1.1 copy-start.5
  573.0 1.1 copy-start.7
  573.0 1.1 copy-start.29
  574.2 5.9 %copy-start.18 = (f32[3,256]{1,0:T(4,128)S(1)}, f32[3,256]{1,0:T(4,128)}, u32[]{:S(2)}) copy-start(f32[3,256]{1,0:T(4,128)} %copy-done.17) | copy-start | bytes 9220
  574.2 5.9 %copy-start.20 = (f32[3,256]{1,0:T(4,128)S(1)}, f32[3,256]{1,0:T(4,128)}, u32[]{:S(2)}) copy-start(f32[3,256]{1,0:T(4,128)} %copy-done.19) | copy-start | bytes 9220
  574.2 5.9 %copy-start.22 = (f32[3,1,256]{2,0,1:T(4,128)S(1)}, f32[3,1,256]{2,0,1:T(4,128)}, u32[]{:S(2)}) copy-start(f32[3,1,256]{2,0,1:T(4,128)} %copy-done.21) | copy-start | bytes 9220
  574.3 5.7 collective-permute-start.9
